TPU v7x, 256 devices: a whole 4x4x8 slice. The times are simulated.
256 devices in a mesh: dp: 32 (over z_lo, y, core), expert: 4 (over x), rollout: 2 (over z_hi).
Axes of the slice: x: 4, y: 4, z: 8 (z_hi: 2, z_lo: 4; z = z_hi * 4 + z_lo), core: 2. Of those that a mesh axis runs over, the one named last changes fastest.
Arguments:
- hidden: bfloat16 [16, 20480, 1536], P('expert', ('dp', 'rollout')), may hold values from -16 to 16
- slot_token: int32 [16, 20480], P('expert', ('dp', 'rollout')), may hold values from 0 to 511, as said below
- gate: float32 [16, 20480], P('expert', ('dp', 'rollout')), may hold values from 0.05 to 1
- counts: int32 [16, 64], P('expert', ('dp', 'rollout')), may hold values from 106 to 320, as said below
- cotangent: bfloat16 [32768, 4096], P(('dp', 'rollout')), may hold values from -0.02734375 to 0.02734375
- halfwidth_replica: bfloat16 [5632, 1024], P(None, 'expert'), may hold values from -0.59765625 to 0.59765625
- precise_matrices: float32 [5632, 1024], P(('dp', 'rollout'), 'expert'), may hold values from -0.6 to 0.6
- running_mean: float32 [5632, 1024], P(('dp', 'rollout'), 'expert'), may hold values from -0.6 to 0.6
- running_variance: float32 [5632, 1024], P(('dp', 'rollout'), 'expert'), may hold values from 0.01 to 1
- base: bfloat16 [16, 1536, 4096], P('expert', 'rollout', 'dp'), may hold values from -0.95703125 to 0.95703125
Outputs:
- merged: bfloat16 [16, 1536, 4096], P('expert', None, 'dp')
- revised_precise: float32 [5632, 1024], P(('dp', 'rollout'), 'expert')
- new_first: float32 [5632, 1024], P(('dp', 'rollout'), 'expert')
- new_second: float32 [5632, 1024], P(('dp', 'rollout'), 'expert')
Inputs may be any that keep to these rules, and one draw needn't show every extreme that they name: Slot s of expert e is live when (s mod 320) < counts[e, s div 320]; in every column of counts some expert has all 320 slots live. `slot_token`: indexes the cotangent rows of the same device group; within each aligned block of 320 slots of one expert on one device all entries are distinct.
All inputs are finite; a program needn't handle non-finite values.
Results may differ from a plain program's by a relative error of at most 0.005.
Values may be sent and summed in bfloat16 or wider, within the bound.
A program may use at most 128 MiB of HBM per device.

v0:
```python
import jax
import jax.numpy as jnp
from jax import lax
from jax.sharding import PartitionSpec as P

STEP = 100


delta_multiplier = 2.0
beta_first = 0.9
beta_second = 0.95
learn_rate = 0.04
decay_rate = 0.01
adam_eps = 1e-08


def adamw_update(derivative_total, precise_matrices, running_mean, running_variance):
    new_first = beta_first * running_mean + (1.0 - beta_first) * derivative_total
    new_second = (
        beta_second * running_variance + (1.0 - beta_second) * derivative_total * derivative_total
    )
    first_hat = new_first / (1.0 - beta_first**STEP)
    second_hat = new_second / (1.0 - beta_second**STEP)
    revised_precise = precise_matrices - learn_rate * (
        first_hat / (jnp.sqrt(second_hat) + adam_eps) + decay_rate * precise_matrices
    )
    return (revised_precise, new_first, new_second)


def body(
    hidden,
    slot_token,
    gate,
    counts,
    cotangent,
    halfwidth_replica,
    precise_matrices,
    running_mean,
    running_variance,
    base,
):
    experts_here, slot_count, hidden_width = hidden.shape
    model_width = cotangent.shape[1]
    factor_rank = halfwidth_replica.shape[1] // experts_here
    live_slots = lax.broadcasted_iota(jnp.int32, (experts_here, slot_count), 1) < counts
    masked = jnp.where(live_slots[:, :, None], hidden, jnp.zeros((), jnp.bfloat16))
    picked = jnp.take(cotangent, slot_token, axis=0)
    routed = (picked.astype(jnp.float32) * gate[:, :, None]).astype(jnp.bfloat16)
    factors = halfwidth_replica.reshape(hidden_width + model_width, experts_here, factor_rank)
    down_proj = jnp.einsum(
        "ecf,fer->ecr", masked, factors[:hidden_width], preferred_element_type=jnp.float32
    ).astype(jnp.bfloat16)
    back_proj = jnp.einsum(
        "ecd,der->ecr", routed, factors[hidden_width:], preferred_element_type=jnp.float32
    ).astype(jnp.bfloat16)
    grad_first = jnp.einsum("ecf,ecr->fer", masked, back_proj, preferred_element_type=jnp.float32)
    grad_second = jnp.einsum("ecd,ecr->der", routed, down_proj, preferred_element_type=jnp.float32)
    gradient_parts = delta_multiplier * jnp.concatenate(
        [
            grad_first.reshape(hidden_width, experts_here * factor_rank),
            grad_second.reshape(model_width, experts_here * factor_rank),
        ],
        axis=0,
    )
    derivative_total = lax.psum_scatter(
        gradient_parts, ("dp", "rollout"), scatter_dimension=0, tiled=True
    )
    revised_precise, new_first, new_second = adamw_update(
        derivative_total, precise_matrices, running_mean, running_variance
    )
    renewed_matrices = lax.all_gather(
        revised_precise.astype(jnp.bfloat16), ("dp", "rollout"), axis=0, tiled=True
    )
    tile_columns = base.shape[2]
    column_start = lax.axis_index("dp") * tile_columns
    fresh_second = lax.dynamic_slice_in_dim(
        renewed_matrices, hidden_width + column_start, tile_columns, 0
    )
    fresh_second = fresh_second.reshape(tile_columns, experts_here, factor_rank)
    half_rows = base.shape[1]
    fresh_first = lax.dynamic_slice_in_dim(
        renewed_matrices, lax.axis_index("rollout") * half_rows, half_rows, 0
    )
    fresh_first = fresh_first.reshape(half_rows, experts_here, factor_rank)
    rank_product = jnp.einsum(
        "fer,der->efd", fresh_first, fresh_second, preferred_element_type=jnp.float32
    )
    combine_tile = (base.astype(jnp.float32) + delta_multiplier * rank_product).astype(jnp.bfloat16)
    merged = lax.all_gather(combine_tile, "rollout", axis=1, tiled=True)
    return (merged, revised_precise, new_first, new_second)


def solution(mesh):
    in_specs = (
        P("expert", ("dp", "rollout"), None),
        P("expert", ("dp", "rollout")),
        P("expert", ("dp", "rollout")),
        P("expert", ("dp", "rollout")),
        P(("dp", "rollout"), None),
        P(None, "expert"),
        P(("dp", "rollout"), "expert"),
        P(("dp", "rollout"), "expert"),
        P(("dp", "rollout"), "expert"),
        P("expert", "rollout", "dp"),
    )
    out_specs = (
        P("expert", None, "dp"),
        P(("dp", "rollout"), "expert"),
        P(("dp", "rollout"), "expert"),
        P(("dp", "rollout"), "expert"),
    )
    return jax.shard_map(body, mesh=mesh, in_specs=in_specs, out_specs=out_specs, check_vma=False)
```

profile of v0, /device:TPU:23, one launch (start us, length us, event | category | flops | bytes accessed | tf_op | source)
XLA Modules:
  0.0 733.2 jit_solution(18243954957880554516)
XLA Ops:
  7.3 0.8 copy-done.7
  8.0 0.1 iota_compare_fusion
  8.1 0.1 reshape.55
  8.2 0.1 slice-done
  8.3 1.2 copy.25
  9.6 2.9 copy.24
  12.5 21.6 %gather_fusion = bf16[1280,4096]{1,0:T(8,128)(2,1)} fusion(bf16[512,4096]{1,0:T(8,128)(2,1)} %param.14, s32[2048]{0:T(1024)S(1)} %pad_clamp_fusion), kind=kCustom, calls=%fused_computation | custom fusion | bytes 20976640 | tf_op jit(solution)/shard_map/jit(_take)/gather | solution.py:47
  34.1 8.4 %fusion.5 = f32[4,64,1536]{2,1,0:T(8,128)} fusion(bf16[4,320,1536]{2,1,0:T(8,128)(2,1)} %param.10, pred[4,320]{1,0:T(4,128)(4,1)S(1)} %get-tuple-element.8, bf16[4096,4,64]{0,2,1:T(8,128)(2,1)S(1)} %bitcast.19, f32[4,320]{1,0:T(4,128)S(1)} %copy-done.9, bf16[4,320,4096]{2,1,0:T(8,128)(2,1)} %bitcast.16, pred[4,320]{1,0:T(4,128)(4,1)S(1)} %get-tuple-element.9), kind=kOutput, calls=%fused_computation.9 | convolution fusion | flops 945766400 | bytes 18095616 | tf_op jit(solution)/shard_map/ecf,ecr->fer/dot_general | solution.py:56
  42.5 8.9 %fusion = f32[4,64,4096]{2,1,0:T(8,128)} fusion(f32[4,320]{1,0:T(4,128)S(1)} %copy-done.9, bf16[4,320,4096]{2,1,0:T(8,128)(2,1)} %bitcast.17, pred[4,320]{1,0:T(4,128)(4,1)S(1)} %get-tuple-element.9, bf16[1536,4,64]{0,2,1:T(8,128)(2,1)S(1)} %bitcast.22, bf16[4,320,1536]{2,1,0:T(8,128)(2,1)} %param.10, pred[4,320]{1,0:T(4,128)(4,1)S(1)} %get-tuple-element.8), kind=kOutput, calls=%fused_computation.2 | convolution fusion | flops 945766400 | bytes 19406336 | tf_op jit(solution)/shard_map/ecd,ecr->der/dot_general | solution.py:57
  51.4 5.7 copy.21
  57.2 0.5 copy.20
  57.6 5.1 maximum_multiply_fusion
  62.7 0.0 all-gather.3.cloned.1.call-start
  62.8 405.6 %reduce-scatter.2.cloned.1.call-done = f32[88,256]{1,0:T(8,128)} async-done(((f32[5632,256]{1,0:T(8,128)}), f32[88,256]{1,0:T(8,128)}) %reduce-scatter.2.cloned.1.call-update) | async-done | bytes 90128 | tf_op jit(solution)/shard_map/reduce_scatter | solution.py:65
  468.4 1.6 fusion.17
  470.0 0.0 all-gather.5.cloned.1.call-start
  470.1 190.4 %all-gather.3.cloned.1.call-done = bf16[5632,256]{1,0:T(8,128)(2,1)} async-done(((bf16[88,256]{1,0:T(8,128)(2,1)}), bf16[5632,256]{1,0:T(8,128)(2,1)}) %all-gather.3.cloned.1.call-update) | async-done | bytes 2883600 | tf_op jit(solution)/shard_map/all_gather | solution.py:71
  660.5 1.0 constant_dynamic-slice_fusion.1
  661.5 0.2 copy.22
  661.7 0.9 constant_dynamic-slice_fusion
  662.5 0.1 copy.23
  662.6 1.3 add_convert_fusion
  664.0 60.0 %all-gather.5.cloned.1.call-done = bf16[4,1536,128]{2,1,0:T(8,128)(2,1)} async-done(((bf16[4,768,128]{2,1,0:T(8,128)(2,1)}), bf16[4,1536,128]{2,1,0:T(8,128)(2,1)}) %all-gather.5.cloned.1.call-update) | async-done | bytes 1572880 | tf_op jit(solution)/shard_map/all_gather | solution.py:89
  724.0 2.7 copy.27
  (28 shorter events, 0.1 us)
Async XLA Ops:
  7.2 1.2 slice-start
  7.2 2.4 slice-start.1
  7.2 0.8 copy-start.7
  7.2 0.8 copy-start.8
  7.2 461.1 %reduce-scatter.2.cloned.1.call-start = ((), (), s32[]{:S(2)}) async-start(), calls=%async_computation.1 | async-start | bytes 5857280 | tf_op jit(solution)/shard_map/reduce_scatter | solution.py:65
  12.5 21.6 %copy-start = (bf16[4096,256]{0,1:T(8,128)(2,1)S(1)}, bf16[4096,256]{0,1:T(8,128)(2,1)}, u32[]{:S(2)}) copy-start(bf16[4096,256]{0,1:T(8,128)(2,1)} %copy.24) | copy-start | bytes 6291460
  12.5 21.6 %copy-start.9 = (f32[4,320]{1,0:T(4,128)S(1)}, f32[4,320]{1,0:T(4,128)}, u32[]{:S(2)}) copy-start(f32[4,320]{1,0:T(4,128)} %param.12) | copy-start | bytes 15364
  34.1 8.4 %copy-start.2 = (bf16[1536,256]{0,1:T(8,128)(2,1)S(1)}, bf16[1536,256]{0,1:T(8,128)(2,1)}, u32[]{:S(2)}) copy-start(bf16[1536,256]{0,1:T(8,128)(2,1)} %copy.25) | copy-start | bytes 2359300
  51.4 5.7 copy-start.1
  62.7 405.7 %copy-start.4 = (f32[88,256]{1,0:T(8,128)S(1)}, f32[88,256]{1,0:T(8,128)}, u32[]{:S(2)}) copy-start(f32[88,256]{1,0:T(8,128)} %param.16) | copy-start | bytes 270340
  62.7 405.7 %copy-start.5 = (f32[88,256]{1,0:T(8,128)S(1)}, f32[88,256]{1,0:T(8,128)}, u32[]{:S(2)}) copy-start(f32[88,256]{1,0:T(8,128)} %param.17) | copy-start | bytes 270340
  62.7 405.7 %copy-start.6 = (f32[88,256]{1,0:T(8,128)S(1)}, f32[88,256]{1,0:T(8,128)}, u32[]{:S(2)}) copy-start(f32[88,256]{1,0:T(8,128)} %param.18) | copy-start | bytes 270340
  62.7 599.9 %copy-start.3 = (bf16[4,768,128]{2,1,0:T(8,128)(2,1)S(1)}, bf16[4,768,128]{2,1,0:T(8,128)(2,1)}, u32[]{:S(2)}) copy-start(bf16[4,768,128]{2,1,0:T(8,128)(2,1)} %param.19) | copy-start | bytes 2359300
  62.7 597.7 %all-gather.3.cloned.1.call-start = ((), (), s32[]{:S(2)}) async-start(), calls=%async_computation.2 | async-start | bytes 2928640 | tf_op jit(solution)/shard_map/all_gather | solution.py:71
  470.0 254.0 %all-gather.5.cloned.1.call-start = ((), (), s32[]{:S(2)}) async-start(), calls=%async_computation.3 | async-start | bytes 2359296 | tf_op jit(solution)/shard_map/all_gather | solution.py:89
Sparse Core Ops, SparseCore 0:
  62.9 405.4 reduce-scatter.1
  470.7 189.6 all-gather.2
  664.1 59.8 all-gather.4
where the time goes:
time: 735 us; the launch traced here: 733 us
  waiting for transfers between devices  656 us (89%)
  local copies, waits for them, and re-layouts  37.8 us (5%)
  matrix products  18.6 us (3%)
  between operations  13.8 us (2%)
    reduce_scatter x1, waiting for transfers between devices, body(): lax.psum_scatter(gradient_parts, ('dp', 'rollout'), scatter_dimension=0,...  406 us
    all_gather x1, waiting for transfers between devices, body(): lax.all_gather(revised_precise.astype(jnp.bfloat16), ('dp', 'rollout'), a...  190 us
    all_gather x1, waiting for transfers between devices, body(): merged = lax.all_gather(combine_tile, 'rollout', axis=1, tiled=True)  60 us
    gather x1, local copies, waits for them, and re-layouts, body(): picked = jnp.take(cotangent, slot_token, axis=0)  21.6 us
  transfers between devices with their start and end apart: 3, of which 3 were waited for; matrix products, arithmetic and copies ran while one was open for 0% of the time, Pallas kernels for 0%

commit v1 on v0

v1 whole, which is shorter than its diff:
```python
import functools

import jax
import jax.numpy as jnp
from jax import lax
from jax.experimental import pallas as pl
from jax.experimental.pallas import tpu as pltpu
from jax.sharding import PartitionSpec as P

STEP = 100

delta_multiplier = 2.0
beta_first = 0.9
beta_second = 0.95
learn_rate = 0.04
decay_rate = 0.01
adam_eps = 1e-08

MESH = pl.DeviceIdType.MESH
BF16 = jnp.bfloat16
F32 = jnp.float32

EXPERTS = 4
CAP = 320
SLOTS = EXPERTS * CAP
INNER = 1536
WIDE = 4096
TOK = 512
COLS = 256
ROWS = INNER + WIDE
SHARD = 88
PAIR = 2 * SHARD
TILE = 512
SPAN = 128
A_BLOCKS = 18


def adamw_update(derivative_total, precise_matrices, running_mean, running_variance):
    new_first = beta_first * running_mean + (1.0 - beta_first) * derivative_total
    new_second = (
        beta_second * running_variance + (1.0 - beta_second) * derivative_total * derivative_total
    )
    first_hat = new_first / (1.0 - beta_first**STEP)
    second_hat = new_second / (1.0 - beta_second**STEP)
    revised_precise = precise_matrices - learn_rate * (
        first_hat / (jnp.sqrt(second_hat) + adam_eps) + decay_rate * precise_matrices
    )
    return (revised_precise, new_first, new_second)


def fold(block):
    return jnp.concatenate([block[:, :128], block[:, 128:]], axis=0)


def unfold(block):
    return jnp.concatenate([block[:SHARD], block[SHARD:]], axis=1)


def dot(lhs, rhs):
    return jnp.dot(lhs, rhs, preferred_element_type=F32)


def dot_t(lhs, rhs):
    return lax.dot_general(lhs, rhs, (((0,), (0,)), ((), ())), preferred_element_type=F32)


def split(value):
    high = value.astype(BF16)
    return high, (value - high.astype(F32)).astype(BF16)


def exchange_kernel(
    hidden,
    slot_token,
    gate,
    counts,
    cotangent,
    factors,
    precise,
    mean,
    variance,
    base,
    base_other,
    fresh_main,
    fresh_extra,
    fresh_second,
    grad_out,
    hid,
    cot,
    fac,
    tok_v,
    gate_v,
    counts_v,
    opt_v,
    select,
    slots_v,
    grad,
    from_core,
    y_send,
    y_recv,
    z_keep,
    z_send,
    z_recv,
    fresh,
    load_sem,
    local_sem,
    base_sem,
    core_send_sem,
    core_recv_sem,
    y_send_sem,
    y_recv_sem,
    z_send_sem,
    z_recv_sem,
    az_send_sem,
    az_recv_sem,
    ay_send_sem,
    ay_recv_sem,
    ac_send_sem,
    ac_recv_sem,
    b_send_sem,
    b_recv_sem,
):
    dp = lax.axis_index("dp")
    half = lax.axis_index("rollout")
    core = lax.rem(dp, 2)
    row = lax.rem(lax.div(dp, 2), 4)
    low = lax.div(dp, 8)
    z = half * 4 + low
    mine = dp * 2 + half

    def device(c, y, zz):
        return {"dp": lax.rem(zz, 4) * 8 + y * 2 + c, "rollout": lax.div(zz, 4)}

    def at_y(step):
        return lax.rem(row + step, 4)

    def at_z(step):
        return lax.rem(z + step, 8)

    def remote(src, dst, send, recv, target):
        return pltpu.make_async_remote_copy(
            src_ref=src,
            dst_ref=dst,
            send_sem=send,
            recv_sem=recv,
            device_id=target,
            device_id_type=MESH,
        )

    loads = []

    def load(src, dst):
        copy = pltpu.make_async_copy(src, dst, load_sem.at[len(loads)])
        copy.start()
        loads.append(copy)
        return copy

    load_a = load(factors.at[pl.ds(0, INNER)], fac.at[pl.ds(0, INNER)])
    load_h = [
        load(hidden.at[e], hid.at[pl.ds(e * CAP, CAP)]) for e in range(EXPERTS)
    ]
    load_small = [load(slot_token, tok_v), load(gate, gate_v), load(counts, counts_v)]
    load_c = load(cotangent, cot)
    load_b = load(factors.at[pl.ds(INNER, WIDE)], fac.at[pl.ds(INNER, WIDE)])
    load_o = [
        load(precise, opt_v.at[0]),
        load(mean, opt_v.at[1]),
        load(variance, opt_v.at[2]),
    ]

    sends = []
    first_row = mine * SHARD - INNER
    first_user = lax.div(jnp.maximum(first_row, 0), SPAN)
    last_user = lax.div(jnp.maximum(first_row + SHARD - 1, 0), SPAN)
    has_second = first_row + SHARD > 0
    for q, user in enumerate((first_user, last_user)):
        wanted = has_second if q == 0 else jnp.logical_and(has_second, last_user != first_user)
        slot = mine - lax.div(INNER + SPAN * user, SHARD)
        for t in range(2):
            own = jnp.logical_and(user == dp, half == t)
            sends.append((user, t, slot, wanted, own))
    first_block = lax.div(INNER + SPAN * dp, SHARD)
    takes = []
    for j in range(3):
        block = first_block + j
        wanted = block * SHARD < INNER + SPAN * dp + SPAN
        takes.append((block, wanted, block == mine))

    barrier = pltpu.get_barrier_semaphore()

    def greet(target):
        pl.semaphore_signal(barrier, inc=1, device_id=target, device_id_type=MESH)

    greet(device(1 - core, row, z))
    for step in range(1, 4):
        greet(device(core, at_y(step), z))
    for step in range(1, 8):
        greet(device(core, row, at_z(step)))
    for user, t, slot, wanted, own in sends:

        @pl.when(jnp.logical_and(wanted, jnp.logical_not(own)))
        def _():
            greet({"dp": user, "rollout": t})

    for block, wanted, own in takes:

        @pl.when(jnp.logical_and(wanted, jnp.logical_not(own)))
        def _():
            greet({"dp": lax.div(block, 2), "rollout": lax.rem(block, 2)})

    greeted = 11
    for wanted, own in [s[3:] for s in sends] + [t[1:] for t in takes]:
        greeted = greeted + jnp.where(jnp.logical_and(wanted, jnp.logical_not(own)), 1, 0)
    pl.semaphore_wait(barrier, greeted)

    base_copy = remote(base, base_other, base_sem.at[0], base_sem.at[1], device(core, row, at_z(4)))
    base_copy.start()

    load_a.wait()
    lanes = lax.broadcasted_iota(jnp.int32, (CAP, COLS), 1)
    for e in range(EXPERTS):
        load_h[e].wait()
        down = dot(hid[e * CAP : (e + 1) * CAP], fac[:INNER])
        inside = jnp.logical_and(lanes >= e * 64, lanes < (e + 1) * 64)
        slots_v[e * CAP : (e + 1) * CAP] = jnp.where(inside, down, 0.0).astype(BF16)
    for copy in load_small:
        copy.wait()
    places = lax.broadcasted_iota(jnp.int32, (EXPERTS, CAP), 1)
    live_gate = jnp.where(places < counts_v[...], gate_v[...], 0.0)
    gate_high = live_gate.astype(BF16).astype(F32)
    gate_low = live_gate - gate_high
    tokens = lax.broadcasted_iota(jnp.int32, (TOK, CAP), 0)
    for e in range(EXPERTS):
        hit = tokens == tok_v[e : e + 1]
        for part, value in enumerate((gate_high, gate_low)):
            select[e, part] = jnp.where(hit, value[e : e + 1], 0.0).astype(BF16)
    by_token = jnp.zeros((TOK, COLS), F32)
    for e in range(EXPERTS):
        down = slots_v[e * CAP : (e + 1) * CAP]
        by_token = by_token + dot(select[e, 0], down) + dot(select[e, 1], down)
    token_high, token_low = split(by_token)

    load_c.wait()
    load_b.wait()
    back_high, back_low = split(dot(cot[...], fac[INNER:]))
    for e in range(EXPERTS):
        inside = jnp.logical_and(lanes >= e * 64, lanes < (e + 1) * 64)
        back = (
            dot_t(select[e, 0], back_high)
            + dot_t(select[e, 1], back_high)
            + dot_t(select[e, 0], back_low)
        )
        slots_v[e * CAP : (e + 1) * CAP] = jnp.where(inside, back, 0.0).astype(BF16)

    def core_copy(chunk):
        return remote(
            grad.at[pl.ds(pl.multiple_of(352 * chunk + PAIR * (1 - core), 8), PAIR)],
            from_core.at[chunk],
            core_send_sem.at[chunk],
            core_recv_sem.at[chunk],
            device(1 - core, row, z),
        )

    def own_rows(chunk):
        return grad[pl.ds(pl.multiple_of(352 * chunk + PAIR * core, 8), PAIR)]

    def y_copy(g, step):
        return remote(
            y_send.at[g, step - 1],
            y_recv.at[g, step - 1],
            y_send_sem.at[g, step - 1],
            y_recv_sem.at[g, step - 1],
            device(core, at_y(step), z),
        )

    def to_core(g):
        for chunk in range(4 * g, 4 * g + 4):
            core_copy(chunk).start()

    def to_y(g):
        for chunk in range(4 * g, 4 * g + 4):
            core_copy(chunk).wait_recv()
        for step in (2, 1, 3):
            chunk = 4 * g + at_y(step)
            y_send[g, step - 1] = (own_rows(chunk) + from_core[chunk]).astype(BF16)
            y_copy(g, step).start()

    for tile in range(3):
        grad[tile * TILE : (tile + 1) * TILE] = dot_t(
            hid[:, tile * TILE : (tile + 1) * TILE], slots_v[...]
        )
    to_core(0)

    def second_tile(tile):
        lhs = cot[:, tile * TILE : (tile + 1) * TILE]
        grad[INNER + tile * TILE : INNER + (tile + 1) * TILE] = dot_t(lhs, token_high) + dot_t(
            lhs, token_low
        )

    for tile in range(0, 3):
        second_tile(tile)
    to_core(1)
    to_y(0)
    for tile in range(3, 6):
        second_tile(tile)
    to_core(2)
    to_y(1)
    for tile in range(6, 8):
        second_tile(tile)
    to_core(3)
    to_y(2)
    to_y(3)

    def z_copy(step_index, block, target):
        return remote(
            z_send.at[block],
            z_recv.at[step_index],
            z_send_sem.at[step_index],
            z_recv_sem.at[step_index],
            device(core, row, target),
        )

    for g in range(4):
        for step in range(1, 4):
            y_copy(g, step).wait_recv()
        chunk = 4 * g + row
        total = own_rows(chunk) + from_core[chunk]
        for step in range(3):
            total = total + y_recv[g, step].astype(F32)
        for h in range(2):
            target = 4 * h + g
            block = fold(total[h * SHARD : (h + 1) * SHARD])
            z_keep[target] = block
            z_send[target] = block.astype(BF16)
            distance = lax.rem(target - z + 8, 8)

            @pl.when(distance != 0)
            def _():
                z_copy(distance - 1, target, target).start()

    derivative = z_keep[z]
    for step in range(1, 8):
        z_copy(step - 1, at_z(step), at_z(step)).wait_recv()
        derivative = derivative + z_recv[step - 1].astype(F32)
    derivative = delta_multiplier * unfold(derivative)
    for copy in load_o:
        copy.wait()
    revised, unused_first, unused_second = adamw_update(derivative, opt_v[0], opt_v[1], opt_v[2])
    fresh[...] = fold(revised).astype(BF16)
    z_keep[0] = fold(derivative)
    grad_copy = pltpu.make_async_copy(z_keep.at[0], grad_out, local_sem.at[5])
    grad_copy.start()

    for q, (user, t, slot, wanted, own) in enumerate(sends):
        copy = remote(
            fresh,
            fresh_second.at[slot],
            b_send_sem.at[q],
            b_recv_sem.at[slot],
            {"dp": user, "rollout": t},
        )

        @pl.when(jnp.logical_and(wanted, jnp.logical_not(own)))
        def _():
            copy.start()

        @pl.when(jnp.logical_and(wanted, own))
        def _():
            local = pltpu.make_async_copy(fresh, fresh_second.at[slot], local_sem.at[0])
            local.start()
            local.wait()

    is_extra = jnp.logical_and(row == 0, core == 0)
    sends_main = low == 0
    sends_extra = jnp.logical_and(low == 1, is_extra)

    def main_place(y, c, h):
        return fresh_main.at[y, c, h]

    def az_copy(step, dst, sem):
        return remote(
            fresh, dst, az_send_sem.at[step - 1], az_recv_sem.at[sem], device(core, row, at_z(step))
        )

    @pl.when(sends_main)
    def _():
        for step in range(1, 8):
            az_copy(step, main_place(row, core, half), half).start()
        local = pltpu.make_async_copy(fresh, main_place(row, core, half), local_sem.at[1])
        local.start()
        local.wait()

    @pl.when(sends_extra)
    def _():
        for step in range(1, 8):
            az_copy(step, fresh_extra.at[half], 2 + half).start()
        local = pltpu.make_async_copy(fresh, fresh_extra.at[half], local_sem.at[2])
        local.start()
        local.wait()

    for h in range(2):

        @pl.when(z != 4 * h)
        def _():
            az_copy(1, main_place(row, core, h), h).wait_recv()

    def ay_copy(y, step):
        return remote(
            fresh_main.at[y, core],
            fresh_main.at[y, core],
            ay_send_sem.at[step - 1],
            ay_recv_sem.at[step - 1],
            device(core, at_y(step), z),
        )

    def ac_copy(y, c):
        return remote(
            fresh_main.at[y, c],
            fresh_main.at[y, c],
            ac_send_sem.at[y],
            ac_recv_sem.at[y],
            device(1 - core, row, z),
        )

    for step in (2, 1, 3):
        ay_copy(row, step).start()
    ac_copy(row, core).start()

    def ey_copy(step):
        return remote(
            fresh_extra,
            fresh_extra,
            ay_send_sem.at[2 + step],
            ay_recv_sem.at[3],
            device(core, at_y(step), z),
        )

    def ec_copy():
        return remote(
            fresh_extra, fresh_extra, ac_send_sem.at[4], ac_recv_sem.at[4], device(1 - core, row, z)
        )

    @pl.when(is_extra)
    def _():
        for h in range(2):

            @pl.when(z != 4 * h + 1)
            def _():
                az_copy(1, fresh_extra.at[h], 2 + h).wait_recv()

        for step in range(1, 4):
            ey_copy(step).start()
        ec_copy().start()

    for step in (1, 3, 2):
        source = lax.rem(row - step + 4, 4)
        ay_copy(source, step).wait_recv()
        ac_copy(source, core).start()

    @pl.when(jnp.logical_and(row != 0, core == 0))
    def _():
        ey_copy(1).wait_recv()
        ec_copy().start()

    for step in range(4):
        ac_copy(at_y(step), 1 - core).wait_recv()

    @pl.when(core == 1)
    def _():
        ec_copy().wait_recv()

    for j, (block, wanted, own) in enumerate(takes):

        @pl.when(jnp.logical_and(wanted, jnp.logical_not(own)))
        def _():
            remote(
                fresh,
                fresh_second.at[j],
                b_send_sem.at[0],
                b_recv_sem.at[j],
                {"dp": lax.div(block, 2), "rollout": lax.rem(block, 2)},
            ).wait_recv()

    for chunk in range(16):
        core_copy(chunk).wait_send()
    for g in range(4):
        for step in range(1, 4):
            y_copy(g, step).wait_send()
    for step in range(1, 8):
        z_copy(step - 1, at_z(step), at_z(step)).wait_send()
    for q, (user, t, slot, wanted, own) in enumerate(sends):

        @pl.when(jnp.logical_and(wanted, jnp.logical_not(own)))
        def _():
            remote(
                fresh,
                fresh_second.at[slot],
                b_send_sem.at[q],
                b_recv_sem.at[slot],
                {"dp": user, "rollout": t},
            ).wait_send()

    @pl.when(jnp.logical_or(sends_main, sends_extra))
    def _():
        for step in range(1, 8):
            az_copy(step, fresh_extra.at[half], 0).wait_send()

    for step in range(1, 4):
        ay_copy(row, step).wait_send()
    for y in range(4):
        ac_copy(y, core).wait_send()

    @pl.when(is_extra)
    def _():
        for step in range(1, 4):
            ey_copy(step).wait_send()

    @pl.when(core == 0)
    def _():
        ec_copy().wait_send()

    grad_copy.wait()
    base_copy.wait()


def exchange(*operands):
    any_space = pl.BlockSpec(memory_space=pl.ANY)
    dma = pltpu.SemaphoreType.DMA
    return pl.pallas_call(
        exchange_kernel,
        out_shape=(
            jax.ShapeDtypeStruct((EXPERTS, INNER // 2, SPAN), BF16),
            jax.ShapeDtypeStruct((4, 2, 2, PAIR, 128), BF16),
            jax.ShapeDtypeStruct((2, PAIR, 128), BF16),
            jax.ShapeDtypeStruct((3, PAIR, 128), BF16),
            jax.ShapeDtypeStruct((PAIR, 128), F32),
        ),
        in_specs=[any_space] * len(operands),
        out_specs=(any_space,) * 5,
        scratch_shapes=[
            pltpu.VMEM((SLOTS, INNER), BF16),
            pltpu.VMEM((TOK, WIDE), BF16),
            pltpu.VMEM((ROWS, COLS), BF16),
            pltpu.VMEM((EXPERTS, CAP), jnp.int32),
            pltpu.VMEM((EXPERTS, CAP), F32),
            pltpu.VMEM((EXPERTS, 1), jnp.int32),
            pltpu.VMEM((3, SHARD, COLS), F32),
            pltpu.VMEM((EXPERTS, 2, TOK, CAP), BF16),
            pltpu.VMEM((SLOTS, COLS), BF16),
            pltpu.VMEM((ROWS, COLS), F32),
            pltpu.VMEM((16, PAIR, COLS), F32),
            pltpu.VMEM((4, 3, PAIR, COLS), BF16),
            pltpu.VMEM((4, 3, PAIR, COLS), BF16),
            pltpu.VMEM((8, PAIR, 128), F32),
            pltpu.VMEM((8, PAIR, 128), BF16),
            pltpu.VMEM((7, PAIR, 128), BF16),
            pltpu.VMEM((PAIR, 128), BF16),
            dma((13,)),
            dma((6,)),
            dma((2,)),
            dma((16,)),
            dma((16,)),
            dma((4, 3)),
            dma((4, 3)),
            dma((7,)),
            dma((7,)),
            dma((7,)),
            dma((4,)),
            dma((6,)),
            dma((4,)),
            dma((5,)),
            dma((5,)),
            dma((4,)),
            dma((3,)),
        ],
        compiler_params=pltpu.CompilerParams(
            collective_id=0, has_side_effects=True, vmem_limit_bytes=56 * 2**20
        ),
    )(*operands)


def merge_kernel(
    base_own,
    base_other,
    fresh_main,
    fresh_extra,
    fresh_second,
    grad_total,
    precise,
    mean,
    variance,
    merged,
    revised_out,
    first_out,
    second_out,
    wide,
    first,
    second,
    near,
):
    e = pl.program_id(0)
    dp = lax.axis_index("dp")
    half = lax.axis_index("rollout")

    @pl.when(e == 0)
    def _():
        for block in range(A_BLOCKS):
            if block < 16:
                folded = fresh_main[block // 4, (block // 2) % 2, block % 2]
            else:
                folded = fresh_extra[block - 16]
            wide[block * SHARD : (block + 1) * SHARD] = unfold(folded.astype(F32))
        first[...] = wide[:INNER].astype(BF16)
        for j in range(3):
            near[j * SHARD : (j + 1) * SHARD] = unfold(fresh_second[j].astype(F32))
        skip = INNER + SPAN * dp - lax.div(INNER + SPAN * dp, SHARD) * SHARD
        second[...] = near[pl.ds(pl.multiple_of(skip, 8), SPAN)].astype(BF16)
        revised, new_first, new_second = adamw_update(
            unfold(grad_total[...]), precise[...], mean[...], variance[...]
        )
        revised_out[...] = revised
        first_out[...] = new_first
        second_out[...] = new_second

    lanes = lax.broadcasted_iota(jnp.int32, (SPAN, COLS), 1)
    inside = jnp.logical_and(lanes >= e * 64, lanes < (e + 1) * 64)
    columns = jnp.where(inside, second[...].astype(F32), 0.0).astype(BF16)
    for part, tile in ((half, base_own), (1 - half, base_other)):
        rows = pl.ds(pl.multiple_of(part * (INNER // 2), 256), INNER // 2)
        product = lax.dot_general(
            first[rows], columns, (((1,), (1,)), ((), ())), preferred_element_type=F32
        )
        merged[0, rows] = (tile[0].astype(F32) + delta_multiplier * product).astype(BF16)


def merge(*operands):
    half_tile = pl.BlockSpec((1, INNER // 2, SPAN), lambda e: (e, 0, 0))

    def whole(shape):
        return pl.BlockSpec(shape, lambda e: (0,) * len(shape))

    shard = whole((SHARD, COLS))
    shard_type = jax.ShapeDtypeStruct((SHARD, COLS), F32)
    return pl.pallas_call(
        merge_kernel,
        grid=(EXPERTS,),
        out_shape=(
            jax.ShapeDtypeStruct((EXPERTS, INNER, SPAN), BF16),
            shard_type,
            shard_type,
            shard_type,
        ),
        in_specs=[
            half_tile,
            half_tile,
            whole((4, 2, 2, PAIR, 128)),
            whole((2, PAIR, 128)),
            whole((3, PAIR, 128)),
            whole((PAIR, 128)),
            shard,
            shard,
            shard,
        ],
        out_specs=(
            pl.BlockSpec((1, INNER, SPAN), lambda e: (e, 0, 0)),
            shard,
            shard,
            shard,
        ),
        scratch_shapes=[
            pltpu.VMEM((A_BLOCKS * SHARD, COLS), F32),
            pltpu.VMEM((INNER, COLS), BF16),
            pltpu.VMEM((SPAN, COLS), BF16),
            pltpu.VMEM((3 * SHARD, COLS), F32),
        ],
        compiler_params=pltpu.CompilerParams(vmem_limit_bytes=32 * 2**20),
    )(*operands)


def body(
    hidden,
    slot_token,
    gate,
    counts,
    cotangent,
    halfwidth_replica,
    precise_matrices,
    running_mean,
    running_variance,
    base,
):
    base_other, fresh_main, fresh_extra, fresh_second, grad_total = exchange(
        hidden,
        slot_token,
        gate,
        counts,
        cotangent,
        halfwidth_replica,
        precise_matrices,
        running_mean,
        running_variance,
        base,
    )
    return merge(
        base,
        base_other,
        fresh_main,
        fresh_extra,
        fresh_second,
        grad_total,
        precise_matrices,
        running_mean,
        running_variance,
    )


def solution(mesh):
    in_specs = (
        P("expert", ("dp", "rollout"), None),
        P("expert", ("dp", "rollout")),
        P("expert", ("dp", "rollout")),
        P("expert", ("dp", "rollout")),
        P(("dp", "rollout"), None),
        P(None, "expert"),
        P(("dp", "rollout"), "expert"),
        P(("dp", "rollout"), "expert"),
        P(("dp", "rollout"), "expert"),
        P("expert", "rollout", "dp"),
    )
    out_specs = (
        P("expert", None, "dp"),
        P(("dp", "rollout"), "expert"),
        P(("dp", "rollout"), "expert"),
        P(("dp", "rollout"), "expert"),
    )
    return jax.shard_map(body, mesh=mesh, in_specs=in_specs, out_specs=out_specs, check_vma=False)
```

time: 735 us -> 81.4 us (0.11)
  waiting for transfers between devices: 656 us -> 0 us
  Pallas kernels: 0 us -> 73 us
  local copies, waits for them, and re-layouts: 37.8 us -> 6.25 us
  matrix products: 18.6 us -> 0 us
  between operations: 13.8 us -> 0.69 us
    reduce_scatter x1 -> x0, waiting for transfers between devices: 406 us -> none  [body(): lax.psum_scatter(gradient_parts, ('dp', 'rollout'), scatter_dimension=0,...]
    all_gather x2 -> x0, waiting for transfers between devices: 250 us -> none  [the longest x1 190 us: body(): lax.all_gather(revised_precise.astype(jnp.bfloat16), ('dp', 'rollout'), a...]
    pallas_call x0 -> x2, Pallas kernels: none -> 73 us  [the longest x1 70.1 us: exchange(): pl.pallas_call(exchange_kernel, out_shape=(jax.ShapeDtypeStruct((EXPERTS,...]
    gather x1 -> x0, local copies, waits for them, and re-layouts: 21.6 us -> none  [body(): picked = jnp.take(cotangent, slot_token, axis=0)]
    dot_general x3 -> x0, matrix products: 18.6 us -> none  [the longest x1 8.94 us: body(): jnp.einsum('ecd,ecr->der', routed, down_proj, preferred_element_type=jnp....]
  transfers between devices with their start and end apart: 3 -> 0, of which waited for: 3 -> 0; matrix products, arithmetic and copies ran while one was open for 0% -> 0% of each run, Pallas kernels for 0% -> 0%
where the time goes in v1:
time: 81.4 us; the launch traced here: 79.9 us
  Pallas kernels  73 us (90%)
  local copies, waits for them, and re-layouts  6.25 us (8%)
    pallas_call x1, Pallas kernels, exchange(): pl.pallas_call(exchange_kernel, out_shape=(jax.ShapeDtypeStruct((EXPERTS,...  70.1 us
    unnamed x19, local copies, waits for them, and re-layouts  6.25 us
    pallas_call x1, Pallas kernels, merge(): pl.pallas_call(merge_kernel, grid=(EXPERTS,), out_shape=(jax.ShapeDtypeSt...  2.85 us

profile of v1, /device:TPU:23, one launch (start us, length us, event | category | flops | bytes accessed | tf_op | source)
XLA Modules:
  0.0 79.9 jit_solution(7681527490523820599)
XLA Ops:
  0.6 1.3 %copy.14.counts = s32[4,1]{1,0:T(4,128)} copy(s32[4,1]{0,1:T(1,128)} %param.13) | data formatting | bytes 32 | tf_op args[3]
  1.9 0.0 copy-start
  1.9 0.0 copy-start.3
  1.9 0.0 copy-start.4
  1.9 0.0 copy-start.5
  2.0 70.1 %shard_map.129 = (bf16[4,768,128]{2,1,0:T(8,128)(2,1)}, bf16[4,2,2,176,128]{4,3,2,1,0:T(8,128)(2,1)}, bf16[2,176,128]{2,1,0:T(8,128)(2,1)}, bf16[3,176,128]{2,1,0:T(8,128)(2,1)}, f32[176,128]{1,0:T(8,128)}) custom-call(bf16[4,320,1536]{2,1,0:T(8,128)(2,1)} %hidden.1, s32[4,320]{1,0:T(4,128)} %slot_token.1, f32[4,320]{1,0:T(4,128)} %gate.1, ...), custom_call_target="tpu_custom_call" | custom-call | tf_op jit(solution)/shard_map/pallas_call | solution.py:529
  72.1 0.0 copy-done
  72.1 0.0 copy-done.3
  72.1 0.0 copy-done.4
  72.1 0.0 copy-done.5
  72.1 0.0 copy-start.1
  72.1 1.1 %copy-done.1 = bf16[4,768,128]{2,1,0:T(8,128)(2,1)S(1)} copy-done((bf16[4,768,128]{2,1,0:T(8,128)(2,1)S(1)}, bf16[4,768,128]{2,1,0:T(8,128)(2,1)}, u32[]{:S(2)}) %copy-start.1) | copy-done | bytes 786456
  73.2 0.0 copy-start.2
  73.2 1.1 %copy-done.2 = bf16[4,2,2,176,128]{4,3,2,1,0:T(8,128)(2,1)S(1)} copy-done((bf16[4,2,2,176,128]{4,3,2,1,0:T(8,128)(2,1)S(1)}, bf16[4,2,2,176,128]{4,3,2,1,0:T(8,128)(2,1)}, u32[]{:S(2)}) %copy-start.2) | copy-done | bytes 720920
  74.3 0.0 copy-start.6
  74.4 0.9 %copy-done.6 = bf16[3,176,128]{2,1,0:T(8,128)(2,1)S(1)} copy-done((bf16[3,176,128]{2,1,0:T(8,128)(2,1)S(1)}, bf16[3,176,128]{2,1,0:T(8,128)(2,1)}, u32[]{:S(2)}) %copy-start.6) | copy-done | bytes 135192
  75.3 0.0 copy-start.7
  75.3 0.9 %copy-done.7 = bf16[2,176,128]{2,1,0:T(8,128)(2,1)S(1)} copy-done((bf16[2,176,128]{2,1,0:T(8,128)(2,1)S(1)}, bf16[2,176,128]{2,1,0:T(8,128)(2,1)}, u32[]{:S(2)}) %copy-start.7) | copy-done | bytes 90136
  76.1 0.0 copy-start.8
  76.1 0.9 %copy-done.8 = f32[176,128]{1,0:T(8,128)S(1)} copy-done((f32[176,128]{1,0:T(8,128)S(1)}, f32[176,128]{1,0:T(8,128)}, u32[]{:S(2)}) %copy-start.8) | copy-done | bytes 90136
  77.0 2.9 %shard_map.130 = (bf16[4,1536,128]{2,1,0:T(8,128)(2,1)}, f32[88,256]{1,0:T(8,128)}, f32[88,256]{1,0:T(8,128)}, f32[88,256]{1,0:T(8,128)}) custom-call(bf16[4,768,128]{2,1,0:T(8,128)(2,1)S(1)} %copy-done, bf16[4,768,128]{2,1,0:T(8,128)(2,1)S(1)} %copy-done.1, bf16[4,2,2,176,128]{4,3,2,1,0:T(8,128)(2,1)S(1)} %copy-done.2, bf16[2,176,128]{2,1,0:T(8,128)(2,1)S(1)} %copy-done.7, ...), custom_call_target="tpu_custom_call" | custom-call | tf_op jit(solution)/shard_map/pallas_call | solution.py:644
Async XLA Ops:
  1.9 70.1 %copy-start = (bf16[4,768,128]{2,1,0:T(8,128)(2,1)S(1)}, bf16[4,768,128]{2,1,0:T(8,128)(2,1)}, u32[]{:S(2)}) copy-start(bf16[4,768,128]{2,1,0:T(8,128)(2,1)} %base_own.1) | copy-start | bytes 2359300
  1.9 70.1 %copy-start.3 = (f32[88,256]{1,0:T(8,128)S(1)}, f32[88,256]{1,0:T(8,128)}, u32[]{:S(2)}) copy-start(f32[88,256]{1,0:T(8,128)} %precise.3) | copy-start | bytes 270340
  1.9 70.1 %copy-start.4 = (f32[88,256]{1,0:T(8,128)S(1)}, f32[88,256]{1,0:T(8,128)}, u32[]{:S(2)}) copy-start(f32[88,256]{1,0:T(8,128)} %mean.3) | copy-start | bytes 270340
  1.9 70.1 %copy-start.5 = (f32[88,256]{1,0:T(8,128)S(1)}, f32[88,256]{1,0:T(8,128)}, u32[]{:S(2)}) copy-start(f32[88,256]{1,0:T(8,128)} %variance.3) | copy-start | bytes 270340
  72.1 1.1 %copy-start.1 = (bf16[4,768,128]{2,1,0:T(8,128)(2,1)S(1)}, bf16[4,768,128]{2,1,0:T(8,128)(2,1)}, u32[]{:S(2)}) copy-start(bf16[4,768,128]{2,1,0:T(8,128)(2,1)} %get-tuple-element.9.base_other) | copy-start | bytes 2359300
  73.2 1.1 %copy-start.2 = (bf16[4,2,2,176,128]{4,3,2,1,0:T(8,128)(2,1)S(1)}, bf16[4,2,2,176,128]{4,3,2,1,0:T(8,128)(2,1)}, u32[]{:S(2)}) copy-start(bf16[4,2,2,176,128]{4,3,2,1,0:T(8,128)(2,1)} %get-tuple-element.10.fresh_main) | copy-start | bytes 2162692
  74.3 0.9 %copy-start.6 = (bf16[3,176,128]{2,1,0:T(8,128)(2,1)S(1)}, bf16[3,176,128]{2,1,0:T(8,128)(2,1)}, u32[]{:S(2)}) copy-start(bf16[3,176,128]{2,1,0:T(8,128)(2,1)} %get-tuple-element.12.fresh_second) | copy-start | bytes 405508
  75.3 0.9 %copy-start.7 = (bf16[2,176,128]{2,1,0:T(8,128)(2,1)S(1)}, bf16[2,176,128]{2,1,0:T(8,128)(2,1)}, u32[]{:S(2)}) copy-start(bf16[2,176,128]{2,1,0:T(8,128)(2,1)} %get-tuple-element.11.fresh_extra) | copy-start | bytes 270340
  76.1 0.9 %copy-start.8 = (f32[176,128]{1,0:T(8,128)S(1)}, f32[176,128]{1,0:T(8,128)}, u32[]{:S(2)}) copy-start(f32[176,128]{1,0:T(8,128)} %get-tuple-element.13.grad_total) | copy-start | bytes 270340

commit v2 on v1

--- a/solution.py
+++ b/solution.py
@@ -33,6 +33,8 @@
 TILE = 512
 SPAN = 128
 A_BLOCKS = 18
+PIECES = 4
+BASE_TURNS = (11, 0, 5)
 
 
 def adamw_update(derivative_total, precise_matrices, running_mean, running_variance):
@@ -104,7 +106,8 @@
     fresh,
     load_sem,
     local_sem,
-    base_sem,
+    base_send_sem,
+    base_recv_sem,
     core_send_sem,
     core_recv_sem,
     y_send_sem,
@@ -155,13 +158,13 @@
         loads.append(copy)
         return copy
 
-    load_a = load(factors.at[pl.ds(0, INNER)], fac.at[pl.ds(0, INNER)])
+    load_c = load(cotangent, cot)
+    load_b = load(factors.at[pl.ds(INNER, WIDE)], fac.at[pl.ds(INNER, WIDE)])
+    load_small = [load(slot_token, tok_v), load(gate, gate_v), load(counts, counts_v)]
     load_h = [
         load(hidden.at[e], hid.at[pl.ds(e * CAP, CAP)]) for e in range(EXPERTS)
     ]
-    load_small = [load(slot_token, tok_v), load(gate, gate_v), load(counts, counts_v)]
-    load_c = load(cotangent, cot)
-    load_b = load(factors.at[pl.ds(INNER, WIDE)], fac.at[pl.ds(INNER, WIDE)])
+    load_a = load(factors.at[pl.ds(0, INNER)], fac.at[pl.ds(0, INNER)])
     load_o = [
         load(precise, opt_v.at[0]),
         load(mean, opt_v.at[1]),
@@ -213,33 +216,36 @@
         greeted = greeted + jnp.where(jnp.logical_and(wanted, jnp.logical_not(own)), 1, 0)
     pl.semaphore_wait(barrier, greeted)
 
-    base_copy = remote(base, base_other, base_sem.at[0], base_sem.at[1], device(core, row, at_z(4)))
-    base_copy.start()
-
-    load_a.wait()
-    lanes = lax.broadcasted_iota(jnp.int32, (CAP, COLS), 1)
-    for e in range(EXPERTS):
-        load_h[e].wait()
-        down = dot(hid[e * CAP : (e + 1) * CAP], fac[:INNER])
-        inside = jnp.logical_and(lanes >= e * 64, lanes < (e + 1) * 64)
-        slots_v[e * CAP : (e + 1) * CAP] = jnp.where(inside, down, 0.0).astype(BF16)
+    def base_copy(piece):
+        rows = INNER // 2 // PIECES
+        place = (piece // PIECES, pl.ds(piece % PIECES * rows, rows))
+        return remote(
+            base.at[place],
+            base_other.at[place],
+            base_send_sem.at[piece],
+            base_recv_sem.at[piece],
+            device(core, row, at_z(4)),
+        )
+
+    def send_base(turn):
+        first = sum(BASE_TURNS[:turn])
+        for piece in range(first, first + BASE_TURNS[turn]):
+            base_copy(piece).start()
+
+    send_base(0)
+
     for copy in load_small:
         copy.wait()
-    places = lax.broadcasted_iota(jnp.int32, (EXPERTS, CAP), 1)
-    live_gate = jnp.where(places < counts_v[...], gate_v[...], 0.0)
-    gate_high = live_gate.astype(BF16).astype(F32)
-    gate_low = live_gate - gate_high
+    places = lax.broadcasted_iota(jnp.int32, (1, CAP), 1)
     tokens = lax.broadcasted_iota(jnp.int32, (TOK, CAP), 0)
     for e in range(EXPERTS):
+        live_gate = jnp.where(places < counts_v[0, e], gate_v[e : e + 1], 0.0)
+        gate_high = live_gate.astype(BF16).astype(F32)
+        gate_low = live_gate - gate_high
         hit = tokens == tok_v[e : e + 1]
         for part, value in enumerate((gate_high, gate_low)):
-            select[e, part] = jnp.where(hit, value[e : e + 1], 0.0).astype(BF16)
-    by_token = jnp.zeros((TOK, COLS), F32)
-    for e in range(EXPERTS):
-        down = slots_v[e * CAP : (e + 1) * CAP]
-        by_token = by_token + dot(select[e, 0], down) + dot(select[e, 1], down)
-    token_high, token_low = split(by_token)
-
+            select[e, part] = jnp.where(hit, value, 0.0).astype(BF16)
+    lanes = lax.broadcasted_iota(jnp.int32, (CAP, COLS), 1)
     load_c.wait()
     load_b.wait()
     back_high, back_low = split(dot(cot[...], fac[INNER:]))
@@ -285,11 +291,23 @@
             y_send[g, step - 1] = (own_rows(chunk) + from_core[chunk]).astype(BF16)
             y_copy(g, step).start()
 
+    for copy in load_h:
+        copy.wait()
     for tile in range(3):
         grad[tile * TILE : (tile + 1) * TILE] = dot_t(
             hid[:, tile * TILE : (tile + 1) * TILE], slots_v[...]
         )
     to_core(0)
+
+    load_a.wait()
+    by_token = jnp.zeros((TOK, COLS), F32)
+    for e in range(EXPERTS):
+        down = dot(hid[e * CAP : (e + 1) * CAP], fac[:INNER])
+        inside = jnp.logical_and(lanes >= e * 64, lanes < (e + 1) * 64)
+        down = jnp.where(inside, down, 0.0).astype(BF16)
+        by_token = by_token + dot(select[e, 0], down) + dot(select[e, 1], down)
+    token_high, token_low = split(by_token)
+    to_y(0)
 
     def second_tile(tile):
         lhs = cot[:, tile * TILE : (tile + 1) * TILE]
@@ -300,7 +318,6 @@
     for tile in range(0, 3):
         second_tile(tile)
     to_core(1)
-    to_y(0)
     for tile in range(3, 6):
         second_tile(tile)
     to_core(2)
@@ -320,7 +337,7 @@
             device(core, row, target),
         )
 
-    for g in range(4):
+    def to_z(g):
         for step in range(1, 4):
             y_copy(g, step).wait_recv()
         chunk = 4 * g + row
@@ -338,21 +355,11 @@
             def _():
                 z_copy(distance - 1, target, target).start()
 
-    derivative = z_keep[z]
-    for step in range(1, 8):
-        z_copy(step - 1, at_z(step), at_z(step)).wait_recv()
-        derivative = derivative + z_recv[step - 1].astype(F32)
-    derivative = delta_multiplier * unfold(derivative)
-    for copy in load_o:
-        copy.wait()
-    revised, unused_first, unused_second = adamw_update(derivative, opt_v[0], opt_v[1], opt_v[2])
-    fresh[...] = fold(revised).astype(BF16)
-    z_keep[0] = fold(derivative)
-    grad_copy = pltpu.make_async_copy(z_keep.at[0], grad_out, local_sem.at[5])
-    grad_copy.start()
-
-    for q, (user, t, slot, wanted, own) in enumerate(sends):
-        copy = remote(
+    grad_copy = pltpu.make_async_copy(z_keep.at[8], grad_out, local_sem.at[5])
+
+    def b_copy(q):
+        user, t, slot = sends[q][:3]
+        return remote(
             fresh,
             fresh_second.at[slot],
             b_send_sem.at[q],
@@ -360,9 +367,25 @@
             {"dp": user, "rollout": t},
         )
 
+    def update():
+        derivative = z_keep[z]
+        for step in range(1, 8):
+            z_copy(step - 1, at_z(step), at_z(step)).wait_recv()
+            derivative = derivative + z_recv[step - 1].astype(F32)
+        derivative = delta_multiplier * derivative
+        z_keep[8] = derivative
+        revised, unused_first, unused_second = adamw_update(
+            unfold(derivative), opt_v[0], opt_v[1], opt_v[2]
+        )
+        fresh[...] = fold(revised).astype(BF16)
+        grad_copy.start()
+
+    def send_second(q):
+        user, t, slot, wanted, own = sends[q]
+
         @pl.when(jnp.logical_and(wanted, jnp.logical_not(own)))
         def _():
-            copy.start()
+            b_copy(q).start()
 
         @pl.when(jnp.logical_and(wanted, own))
         def _():
@@ -382,7 +405,14 @@
             fresh, dst, az_send_sem.at[step - 1], az_recv_sem.at[sem], device(core, row, at_z(step))
         )
 
-    @pl.when(sends_main)
+    for copy in load_o:
+        copy.wait()
+    for g in range(4):
+        to_z(g)
+    send_base(1)
+    update()
+
+    @pl.when(low == 0)
     def _():
         for step in range(1, 8):
             az_copy(step, main_place(row, core, half), half).start()
@@ -397,6 +427,11 @@
         local = pltpu.make_async_copy(fresh, fresh_extra.at[half], local_sem.at[2])
         local.start()
         local.wait()
+
+    for q in range(len(sends)):
+        send_second(q)
+
+    send_base(2)
 
     for h in range(2):
 
@@ -492,13 +527,7 @@
 
         @pl.when(jnp.logical_and(wanted, jnp.logical_not(own)))
         def _():
-            remote(
-                fresh,
-                fresh_second.at[slot],
-                b_send_sem.at[q],
-                b_recv_sem.at[slot],
-                {"dp": user, "rollout": t},
-            ).wait_send()
+            b_copy(q).wait_send()
 
     @pl.when(jnp.logical_or(sends_main, sends_extra))
     def _():
@@ -520,7 +549,8 @@
         ec_copy().wait_send()
 
     grad_copy.wait()
-    base_copy.wait()
+    for piece in range(EXPERTS * PIECES):
+        base_copy(piece).wait()
 
 
 def exchange(*operands):
@@ -543,7 +573,7 @@
             pltpu.VMEM((ROWS, COLS), BF16),
             pltpu.VMEM((EXPERTS, CAP), jnp.int32),
             pltpu.VMEM((EXPERTS, CAP), F32),
-            pltpu.VMEM((EXPERTS, 1), jnp.int32),
+            pltpu.SMEM((1, EXPERTS), jnp.int32),
             pltpu.VMEM((3, SHARD, COLS), F32),
             pltpu.VMEM((EXPERTS, 2, TOK, CAP), BF16),
             pltpu.VMEM((SLOTS, COLS), BF16),
@@ -551,13 +581,14 @@
             pltpu.VMEM((16, PAIR, COLS), F32),
             pltpu.VMEM((4, 3, PAIR, COLS), BF16),
             pltpu.VMEM((4, 3, PAIR, COLS), BF16),
-            pltpu.VMEM((8, PAIR, 128), F32),
+            pltpu.VMEM((9, PAIR, 128), F32),
             pltpu.VMEM((8, PAIR, 128), BF16),
             pltpu.VMEM((7, PAIR, 128), BF16),
             pltpu.VMEM((PAIR, 128), BF16),
             dma((13,)),
             dma((6,)),
-            dma((2,)),
+            dma((EXPERTS * PIECES,)),
+            dma((EXPERTS * PIECES,)),
             dma((16,)),
             dma((16,)),
             dma((4, 3)),
@@ -673,7 +704,7 @@
             pltpu.VMEM((SPAN, COLS), BF16),
             pltpu.VMEM((3 * SHARD, COLS), F32),
         ],
-        compiler_params=pltpu.CompilerParams(vmem_limit_bytes=32 * 2**20),
+        compiler_params=pltpu.CompilerParams(vmem_limit_bytes=56 * 2**20),
     )(*operands)
 
 
@@ -693,7 +724,7 @@
         hidden,
         slot_token,
         gate,
-        counts,
+        counts.reshape(1, EXPERTS),
         cotangent,
         halfwidth_replica,
         precise_matrices,

time: 81.4 us -> 68.9 us (0.85); the launches traced: 79.9 us -> 68.8 us
  local copies, waits for them, and re-layouts: 6.25 us -> 0 us
  Pallas kernels: 73 us -> 68.1 us
    pallas_call x1, Pallas kernels: 70.1 us -> 63.1 us  [exchange(): pl.pallas_call(exchange_kernel, out_shape=(jax.ShapeDtypeStruct((EXPERTS,...]
    unnamed x19 -> x0, local copies, waits for them, and re-layouts: 6.25 us -> none
    pallas_call x1, Pallas kernels: 2.85 us -> 5.04 us  [merge(): pl.pallas_call(merge_kernel, grid=(EXPERTS,), out_shape=(jax.ShapeDtypeSt...]
where the time goes in v2:
time: 68.9 us; the launch traced here: 68.8 us
  Pallas kernels  68.1 us (99%)
    pallas_call x1, Pallas kernels, exchange(): pl.pallas_call(exchange_kernel, out_shape=(jax.ShapeDtypeStruct((EXPERTS,...  63.1 us
    pallas_call x1, Pallas kernels, merge(): pl.pallas_call(merge_kernel, grid=(EXPERTS,), out_shape=(jax.ShapeDtypeSt...  5.04 us

profile of v2, /device:TPU:23, one launch (start us, length us, event | category | flops | bytes accessed | tf_op | source)
XLA Modules:
  0.0 68.8 jit_solution(5724405886841298554)
XLA Ops:
  0.6 63.1 %shard_map.129 = (bf16[4,768,128]{2,1,0:T(8,128)(2,1)}, bf16[4,2,2,176,128]{4,3,2,1,0:T(8,128)(2,1)}, bf16[2,176,128]{2,1,0:T(8,128)(2,1)}, bf16[3,176,128]{2,1,0:T(8,128)(2,1)}, f32[176,128]{1,0:T(8,128)}) custom-call(bf16[4,320,1536]{2,1,0:T(8,128)(2,1)} %hidden.1, s32[4,320]{1,0:T(4,128)} %slot_token.1, f32[4,320]{1,0:T(4,128)} %gate.1, s32[1,4]{1,0:T(1,128)} %bitcast.1, ...), custom_call_target="tpu_custom_call" | custom-call | tf_op jit(solution)/shard_map/pallas_call | solution.py:559
  63.7 5.0 %shard_map.130 = (bf16[4,1536,128]{2,1,0:T(8,128)(2,1)}, f32[88,256]{1,0:T(8,128)}, f32[88,256]{1,0:T(8,128)}, f32[88,256]{1,0:T(8,128)}) custom-call(bf16[4,768,128]{2,1,0:T(8,128)(2,1)} %base_own.1, bf16[4,768,128]{2,1,0:T(8,128)(2,1)} %get-tuple-element.9.base_other, bf16[4,2,2,176,128]{4,3,2,1,0:T(8,128)(2,1)} %get-tuple-element.10.fresh_main, ...), custom_call_target="tpu_custom_call" | custom-call | tf_op jit(solution)/shard_map/pallas_call | solution.py:675

commit v3 on v2

--- a/solution.py
+++ b/solution.py
@@ -270,26 +270,37 @@
     def own_rows(chunk):
         return grad[pl.ds(pl.multiple_of(352 * chunk + PAIR * core, 8), PAIR)]
 
-    def y_copy(g, step):
-        return remote(
-            y_send.at[g, step - 1],
-            y_recv.at[g, step - 1],
-            y_send_sem.at[g, step - 1],
-            y_recv_sem.at[g, step - 1],
-            device(core, at_y(step), z),
+    side = 1 - 2 * core
+
+    def y_copy(g, slot):
+        way = -side if slot == 1 else side
+        return remote(
+            y_send.at[g, slot],
+            y_recv.at[g, slot],
+            y_send_sem.at[g, slot],
+            y_recv_sem.at[g, slot],
+            device(core, at_y(way + 4), z),
         )
 
     def to_core(g):
         for chunk in range(4 * g, 4 * g + 4):
             core_copy(chunk).start()
 
+    def core_sum(g, step):
+        chunk = 4 * g + at_y(step)
+        return own_rows(chunk) + from_core[chunk]
+
     def to_y(g):
         for chunk in range(4 * g, 4 * g + 4):
             core_copy(chunk).wait_recv()
-        for step in (2, 1, 3):
-            chunk = 4 * g + at_y(step)
-            y_send[g, step - 1] = (own_rows(chunk) + from_core[chunk]).astype(BF16)
-            y_copy(g, step).start()
+        for slot, step in ((0, 2), (1, 4 - side)):
+            y_send[g, slot] = core_sum(g, step).astype(BF16)
+            y_copy(g, slot).start()
+
+    def on_along_y(g):
+        y_copy(g, 0).wait_recv()
+        y_send[g, 2] = (core_sum(g, 4 + side) + y_recv[g, 0].astype(F32)).astype(BF16)
+        y_copy(g, 2).start()
 
     for copy in load_h:
         copy.wait()
@@ -322,11 +333,15 @@
         second_tile(tile)
     to_core(2)
     to_y(1)
+    on_along_y(0)
     for tile in range(6, 8):
         second_tile(tile)
     to_core(3)
     to_y(2)
+    on_along_y(1)
     to_y(3)
+    on_along_y(2)
+    on_along_y(3)
 
     def z_copy(step_index, block, target):
         return remote(
@@ -338,12 +353,10 @@
         )
 
     def to_z(g):
-        for step in range(1, 4):
-            y_copy(g, step).wait_recv()
-        chunk = 4 * g + row
-        total = own_rows(chunk) + from_core[chunk]
-        for step in range(3):
-            total = total + y_recv[g, step].astype(F32)
+        total = core_sum(g, 0)
+        for slot in (1, 2):
+            y_copy(g, slot).wait_recv()
+            total = total + y_recv[g, slot].astype(F32)
         for h in range(2):
             target = 4 * h + g
             block = fold(total[h * SHARD : (h + 1) * SHARD])
@@ -519,8 +532,8 @@
     for chunk in range(16):
         core_copy(chunk).wait_send()
     for g in range(4):
-        for step in range(1, 4):
-            y_copy(g, step).wait_send()
+        for slot in range(3):
+            y_copy(g, slot).wait_send()
     for step in range(1, 8):
         z_copy(step - 1, at_z(step), at_z(step)).wait_send()
     for q, (user, t, slot, wanted, own) in enumerate(sends):
@@ -559,11 +572,11 @@
     return pl.pallas_call(
         exchange_kernel,
         out_shape=(
-            jax.ShapeDtypeStruct((EXPERTS, INNER // 2, SPAN), BF16),
-            jax.ShapeDtypeStruct((4, 2, 2, PAIR, 128), BF16),
-            jax.ShapeDtypeStruct((2, PAIR, 128), BF16),
-            jax.ShapeDtypeStruct((3, PAIR, 128), BF16),
-            jax.ShapeDtypeStruct((PAIR, 128), F32),
+            pltpu.VMEM((EXPERTS, INNER // 2, SPAN), BF16),
+            pltpu.VMEM((4, 2, 2, PAIR, 128), BF16),
+            pltpu.VMEM((2, PAIR, 128), BF16),
+            pltpu.VMEM((3, PAIR, 128), BF16),
+            pltpu.VMEM((PAIR, 128), F32),
         ),
         in_specs=[any_space] * len(operands),
         out_specs=(any_space,) * 5,
@@ -605,7 +618,7 @@
             dma((3,)),
         ],
         compiler_params=pltpu.CompilerParams(
-            collective_id=0, has_side_effects=True, vmem_limit_bytes=56 * 2**20
+            collective_id=0, has_side_effects=True, vmem_limit_bytes=60 * 2**20
         ),
     )(*operands)
 
@@ -704,7 +717,7 @@
             pltpu.VMEM((SPAN, COLS), BF16),
             pltpu.VMEM((3 * SHARD, COLS), F32),
         ],
-        compiler_params=pltpu.CompilerParams(vmem_limit_bytes=56 * 2**20),
+        compiler_params=pltpu.CompilerParams(vmem_limit_bytes=32 * 2**20),
     )(*operands)
 
 

time: 68.9 us -> 66.3 us (0.962)
  the two profiles are of different devices: /device:TPU:23 before, /device:TPU:68 now
where the time goes in v3:
time: 66.3 us; the launch traced here: 66.2 us
  Pallas kernels  65.5 us (99%)
  between operations  0.71 us (1%)
    pallas_call x1, Pallas kernels, exchange(): pl.pallas_call(exchange_kernel, out_shape=(pltpu.VMEM((EXPERTS, INNER //...  62.6 us
    pallas_call x1, Pallas kernels, merge(): pl.pallas_call(merge_kernel, grid=(EXPERTS,), out_shape=(jax.ShapeDtypeSt...  2.9 us

profile of v3, /device:TPU:68, one launch (start us, length us, event | category | flops | bytes accessed | tf_op | source)
XLA Modules:
  0.0 66.2 jit_solution(4917339556263449608)
XLA Ops:
  0.6 0.0 copy-start
  0.6 0.0 copy-start.1
  0.7 0.0 copy-start.2
  0.7 0.0 copy-start.3
  0.7 62.6 %shard_map.129 = (bf16[4,768,128]{2,1,0:T(8,128)(2,1)S(1)}, bf16[4,2,2,176,128]{4,3,2,1,0:T(8,128)(2,1)S(1)}, bf16[2,176,128]{2,1,0:T(8,128)(2,1)S(1)}, bf16[3,176,128]{2,1,0:T(8,128)(2,1)S(1)}, f32[176,128]{1,0:T(8,128)S(1)}) custom-call(bf16[4,320,1536]{2,1,0:T(8,128)(2,1)} %hidden.1, s32[4,320]{1,0:T(4,128)} %slot_token.1, f32[4,320]{1,0:T(4,128)} %gate.1, ...), custom_call_target="tpu_custom_call" | custom-call | tf_op jit(solution)/shard_map/pallas_call | solution.py:572
  63.3 0.0 copy-done
  63.3 0.0 copy-done.1
  63.3 0.0 copy-done.2
  63.3 0.0 copy-done.3
  63.3 2.9 %shard_map.130 = (bf16[4,1536,128]{2,1,0:T(8,128)(2,1)}, f32[88,256]{1,0:T(8,128)}, f32[88,256]{1,0:T(8,128)}, f32[88,256]{1,0:T(8,128)}) custom-call(bf16[4,768,128]{2,1,0:T(8,128)(2,1)S(1)} %copy-done, bf16[4,768,128]{2,1,0:T(8,128)(2,1)S(1)} %get-tuple-element.9.base_other, bf16[4,2,2,176,128]{4,3,2,1,0:T(8,128)(2,1)S(1)} %get-tuple-element.10.fresh_main, ...), custom_call_target="tpu_custom_call" | custom-call | tf_op jit(solution)/shard_map/pallas_call | solution.py:688
Async XLA Ops:
  0.6 62.7 %copy-start = (bf16[4,768,128]{2,1,0:T(8,128)(2,1)S(1)}, bf16[4,768,128]{2,1,0:T(8,128)(2,1)}, u32[]{:S(2)}) copy-start(bf16[4,768,128]{2,1,0:T(8,128)(2,1)} %base_own.1) | copy-start | bytes 2359300
  0.6 62.7 %copy-start.1 = (f32[88,256]{1,0:T(8,128)S(1)}, f32[88,256]{1,0:T(8,128)}, u32[]{:S(2)}) copy-start(f32[88,256]{1,0:T(8,128)} %precise.3) | copy-start | bytes 270340
  0.7 62.7 %copy-start.2 = (f32[88,256]{1,0:T(8,128)S(1)}, f32[88,256]{1,0:T(8,128)}, u32[]{:S(2)}) copy-start(f32[88,256]{1,0:T(8,128)} %mean.3) | copy-start | bytes 270340
  0.7 62.7 %copy-start.3 = (f32[88,256]{1,0:T(8,128)S(1)}, f32[88,256]{1,0:T(8,128)}, u32[]{:S(2)}) copy-start(f32[88,256]{1,0:T(8,128)} %variance.3) | copy-start | bytes 270340

commit v4 on v3

--- a/solution.py
+++ b/solution.py
@@ -362,11 +362,6 @@
             block = fold(total[h * SHARD : (h + 1) * SHARD])
             z_keep[target] = block
             z_send[target] = block.astype(BF16)
-            distance = lax.rem(target - z + 8, 8)
-
-            @pl.when(distance != 0)
-            def _():
-                z_copy(distance - 1, target, target).start()
 
     grad_copy = pltpu.make_async_copy(z_keep.at[8], grad_out, local_sem.at[5])
 
@@ -422,6 +417,8 @@
         copy.wait()
     for g in range(4):
         to_z(g)
+    for step in (4, 3, 5, 2, 6, 1, 7):
+        z_copy(step - 1, at_z(step), at_z(step)).start()
     send_base(1)
     update()
 

time: 66.3 us -> 74.7 us (1.13)
  the two profiles are of different devices: /device:TPU:68 before, /device:TPU:23 now
where the time goes in v4:
time: 74.7 us; the launch traced here: 73.7 us
  Pallas kernels  73 us (98%)
    pallas_call x1, Pallas kernels, exchange(): pl.pallas_call(exchange_kernel, out_shape=(pltpu.VMEM((EXPERTS, INNER //...  70.1 us
    pallas_call x1, Pallas kernels, merge(): pl.pallas_call(merge_kernel, grid=(EXPERTS,), out_shape=(jax.ShapeDtypeSt...  2.88 us

profile of v4, /device:TPU:23, one launch (start us, length us, event | category | flops | bytes accessed | tf_op | source)
XLA Modules:
  0.0 73.7 jit_solution(11791542032594763686)
XLA Ops:
  0.6 0.0 copy-start
  0.6 0.0 copy-start.1
  0.7 0.0 copy-start.2
  0.7 0.0 copy-start.3
  0.7 70.1 %shard_map.129 = (bf16[4,768,128]{2,1,0:T(8,128)(2,1)S(1)}, bf16[4,2,2,176,128]{4,3,2,1,0:T(8,128)(2,1)S(1)}, bf16[2,176,128]{2,1,0:T(8,128)(2,1)S(1)}, bf16[3,176,128]{2,1,0:T(8,128)(2,1)S(1)}, f32[176,128]{1,0:T(8,128)S(1)}) custom-call(bf16[4,320,1536]{2,1,0:T(8,128)(2,1)} %hidden.1, s32[4,320]{1,0:T(4,128)} %slot_token.1, f32[4,320]{1,0:T(4,128)} %gate.1, ...), custom_call_target="tpu_custom_call" | custom-call | tf_op jit(solution)/shard_map/pallas_call | solution.py:569
  70.8 0.0 copy-done
  70.8 0.0 copy-done.1
  70.8 0.0 copy-done.2
  70.8 0.0 copy-done.3
  70.8 2.9 %shard_map.130 = (bf16[4,1536,128]{2,1,0:T(8,128)(2,1)}, f32[88,256]{1,0:T(8,128)}, f32[88,256]{1,0:T(8,128)}, f32[88,256]{1,0:T(8,128)}) custom-call(bf16[4,768,128]{2,1,0:T(8,128)(2,1)S(1)} %copy-done, bf16[4,768,128]{2,1,0:T(8,128)(2,1)S(1)} %get-tuple-element.9.base_other, bf16[4,2,2,176,128]{4,3,2,1,0:T(8,128)(2,1)S(1)} %get-tuple-element.10.fresh_main, ...), custom_call_target="tpu_custom_call" | custom-call | tf_op jit(solution)/shard_map/pallas_call | solution.py:685
Async XLA Ops:
  0.6 70.2 %copy-start = (bf16[4,768,128]{2,1,0:T(8,128)(2,1)S(1)}, bf16[4,768,128]{2,1,0:T(8,128)(2,1)}, u32[]{:S(2)}) copy-start(bf16[4,768,128]{2,1,0:T(8,128)(2,1)} %base_own.1) | copy-start | bytes 2359300
  0.6 70.2 %copy-start.1 = (f32[88,256]{1,0:T(8,128)S(1)}, f32[88,256]{1,0:T(8,128)}, u32[]{:S(2)}) copy-start(f32[88,256]{1,0:T(8,128)} %precise.3) | copy-start | bytes 270340
  0.7 70.2 %copy-start.2 = (f32[88,256]{1,0:T(8,128)S(1)}, f32[88,256]{1,0:T(8,128)}, u32[]{:S(2)}) copy-start(f32[88,256]{1,0:T(8,128)} %mean.3) | copy-start | bytes 270340
  0.7 70.2 %copy-start.3 = (f32[88,256]{1,0:T(8,128)S(1)}, f32[88,256]{1,0:T(8,128)}, u32[]{:S(2)}) copy-start(f32[88,256]{1,0:T(8,128)} %variance.3) | copy-start | bytes 270340
